TPU v7x, 32 devices: a whole 2x2x4 slice. The times are simulated.
32 devices in a mesh: frame: 8 (over y, x, core), row: 4 (over z).
Axes of the slice: x: 2, y: 2, z: 4, core: 2. Of those that a mesh axis runs over, the one named last changes fastest.
Arguments:
- clip: bfloat16 [16, 48, 128, 320], P('frame', 'row'), may hold values from -6 to 6
- w_spatial: bfloat16 [3, 3, 320, 320], replicated, may hold values from -0.109375 to 0.109375
- b_spatial: float32 [320], replicated, may hold values from -3 to 3
- w_temporal: bfloat16 [3, 320, 320], replicated, may hold values from -0.1875 to 0.1875
- b_temporal: float32 [320], replicated, may hold values from -3 to 3
- ln_gain: float32 [320], replicated, may hold values from 0.1 to 1.9
- ln_bias: float32 [320], replicated, may hold values from -3 to 3
- w_query: bfloat16 [320, 320], replicated, may hold values from -1.677051 to 1.677051
- w_key: bfloat16 [320, 320], replicated, may hold values from -1.677051 to 1.677051
- w_value: bfloat16 [320, 320], replicated, may hold values from -0.3125 to 0.3125
- w_out: bfloat16 [320, 320], replicated, may hold values from -0.3125 to 0.3125
- b_out: float32 [320], replicated, may hold values from -3 to 3
Outputs:
- mixed: bfloat16 [16, 48, 128, 320], P('frame', 'row')
All inputs are finite; a program needn't handle non-finite values.
Results may differ from a plain program's by a relative error of at most 0.0062.
Values may be sent and summed in bfloat16 or wider, within the bound.
A program may use at most 128 MiB of HBM per device.

v0:
```python
import functools

import jax
import jax.numpy as jnp
from jax import lax
from jax.experimental import pallas as pl
from jax.experimental.pallas import tpu as pltpu
from jax.sharding import PartitionSpec as P

HEAD = 64


def extended(block, sides, width):
    for axis, dim in sides:
        count = lax.axis_size(axis)
        forward = [(i, i + 1) for i in range(count - 1)]
        backward = [(target, source) for source, target in forward]
        low = lax.ppermute(
            lax.slice_in_dim(block, block.shape[dim] - width, None, axis=dim), axis, forward
        )
        high = lax.ppermute(lax.slice_in_dim(block, 0, width, axis=dim), axis, backward)
        block = jnp.concatenate([low, block, high], axis=dim)
    return block


def temporal_conv(padded, w_temporal, b_temporal):
    count = padded.shape[0] - 2
    total = padded[1 : 1 + count].astype(jnp.float32) + b_temporal
    for tap in range(3):
        total = total + jnp.einsum(
            "frwc,co->frwo",
            padded[tap : tap + count],
            w_temporal[tap],
            preferred_element_type=jnp.float32,
        )
    return total.astype(jnp.bfloat16)


def attend_back(framed, ln_gain, ln_bias, w_query, w_key, w_value, w_out, b_out):
    frames, rows, cols, width = framed.shape
    values32 = framed.astype(jnp.float32)
    center = jnp.mean(values32, axis=-1, keepdims=True)
    spread = jnp.mean((values32 - center) ** 2, axis=-1, keepdims=True)
    normed = ((values32 - center) * lax.rsqrt(spread + 1e-05) * ln_gain + ln_bias).astype(
        jnp.bfloat16
    )
    query = jnp.einsum("frwc,cd->frwd", normed, w_query, preferred_element_type=jnp.float32).astype(
        jnp.bfloat16
    )
    key_rows = jnp.einsum(
        "frwc,cd->frwd", normed, w_key, preferred_element_type=jnp.float32
    ).astype(jnp.bfloat16)
    value = jnp.einsum("frwc,cd->frwd", normed, w_value, preferred_element_type=jnp.float32).astype(
        jnp.bfloat16
    )
    heads = width // HEAD
    query = query.reshape(frames, rows, cols, heads, HEAD)
    key_rows = key_rows.reshape(frames, rows, cols, heads, HEAD)
    value = value.reshape(frames, rows, cols, heads, HEAD)
    scores = jnp.einsum(
        "frwhd,grwhd->rwhfg", query, key_rows, preferred_element_type=jnp.float32
    ) / jnp.sqrt(jnp.float32(HEAD))
    top = jnp.max(scores, axis=-1, keepdims=True)
    raised = jnp.exp(scores - top)
    weights = (raised / jnp.sum(raised, axis=-1, keepdims=True)).astype(jnp.bfloat16)
    attended = jnp.einsum("rwhfg,grwhd->frwhd", weights, value, preferred_element_type=jnp.float32)
    attended = attended.reshape(frames, rows, cols, width).astype(jnp.bfloat16)
    result = (
        values32
        + jnp.einsum("frwc,co->frwo", attended, w_out, preferred_element_type=jnp.float32)
        + b_out
    )
    result = result.astype(jnp.bfloat16)
    return lax.all_to_all(result, "frame", split_axis=0, concat_axis=2, tiled=True)


def on_device(
    clip,
    w_spatial,
    b_spatial,
    w_temporal,
    b_temporal,
    ln_gain,
    ln_bias,
    w_query,
    w_key,
    w_value,
    w_out,
    b_out,
):
    rows = clip.shape[1]
    cols = clip.shape[2]
    padded = extended(clip, (("row", 1),), 1)
    padded = jnp.pad(padded, ((0, 0), (0, 0), (1, 1), (0, 0)))
    total = jnp.zeros(clip.shape, jnp.float32) + b_spatial
    for tap_row in range(3):
        for tap_col in range(3):
            window = padded[:, tap_row : tap_row + rows, tap_col : tap_col + cols]
            total = total + jnp.einsum(
                "frwc,co->frwo",
                window,
                w_spatial[tap_row, tap_col],
                preferred_element_type=jnp.float32,
            )
    spatial = total.astype(jnp.bfloat16)
    zero_rim = jnp.pad(
        lax.all_to_all(spatial, "frame", split_axis=2, concat_axis=0, tiled=True),
        ((1, 1), (0, 0), (0, 0), (0, 0)),
    )
    framed = temporal_conv(zero_rim, w_temporal, b_temporal)
    return attend_back(framed, ln_gain, ln_bias, w_query, w_key, w_value, w_out, b_out)


MESH = pl.DeviceIdType.MESH
F32 = jnp.float32
BF16 = jnp.bfloat16
PARTS = 4


def down(x, count):
    return jnp.concatenate([jnp.zeros((count, x.shape[1]), x.dtype), x[:-count]], axis=0)


def up(x, count):
    return jnp.concatenate([x[count:], jnp.zeros((count, x.shape[1]), x.dtype)], axis=0)


def dot(a, b):
    return jnp.dot(a, b, preferred_element_type=F32)


def fused(
    n, nrow, clip, ws, bs, wt, bt, gain, lbias, wqkv, wo, bo, out,
    xp, snd, rcv, osnd, orcv, load_sem, hsend, hrecv, s1, r1, s2, r2,
):
    me = lax.axis_index("frame")
    zi = lax.axis_index("row")
    rows = clip.shape[1]
    per = rows // PARTS
    above = lax.rem(zi + 1, nrow)
    below = lax.rem(zi + nrow - 1, nrow)

    load = pltpu.make_async_copy(clip, xp.at[:, pl.ds(1, rows)], load_sem)
    load.start()

    barrier = pltpu.get_barrier_semaphore()

    def greet(k, _):
        pl.semaphore_signal(
            barrier, inc=1, device_id={"frame": lax.rem(me + k, n)}, device_id_type=MESH
        )
        return 0

    lax.fori_loop(1, n, greet, 0)
    pl.semaphore_signal(barrier, inc=1, device_id={"row": above}, device_id_type=MESH)
    pl.semaphore_signal(barrier, inc=1, device_id={"row": below}, device_id_type=MESH)
    pl.semaphore_wait(barrier, n + 1)

    to_above = pltpu.make_async_remote_copy(
        src_ref=clip.at[:, rows - 1], dst_ref=xp.at[:, 0],
        send_sem=hsend.at[0], recv_sem=hrecv.at[0],
        device_id={"row": above}, device_id_type=MESH,
    )
    to_below = pltpu.make_async_remote_copy(
        src_ref=clip.at[:, 0], dst_ref=xp.at[:, rows + 1],
        send_sem=hsend.at[1], recv_sem=hrecv.at[1],
        device_id={"row": below}, device_id_type=MESH,
    )
    to_above.start()
    to_below.start()
    load.wait()

    def move(buf, land, ss, rs, part, k):
        peer = lax.rem(me + k, n)
        span = pl.ds(part * per, per)
        return pltpu.make_async_remote_copy(
            src_ref=buf.at[peer, span], dst_ref=land.at[me, span],
            send_sem=ss.at[part, k], recv_sem=rs.at[part, k],
            device_id={"frame": peer}, device_id_type=MESH,
        )

    def arrived(buf, land, ss, rs, part, k):
        source = lax.rem(me + n - k, n)
        span = pl.ds(part * per, per)
        return pltpu.make_async_remote_copy(
            src_ref=buf.at[source, span], dst_ref=land.at[source, span],
            send_sem=ss.at[part, k], recv_sem=rs.at[part, k],
            device_id={"frame": source}, device_id_type=MESH,
        )

    def send_all(buf, land, ss, rs, part):
        def one(k, _):
            move(buf, land, ss, rs, part, k).start()
            return 0
        lax.fori_loop(1, n, one, 0)
        span = pl.ds(part * per, per)
        land[me, span] = buf[me, span]

    def recv_all(buf, land, ss, rs, part):
        def one(k, _):
            arrived(buf, land, ss, rs, part, k).wait_recv()
            return 0
        lax.fori_loop(1, n, one, 0)

    def drain(buf, land, ss, rs):
        def one(i, _):
            move(buf, land, ss, rs, i // (n - 1), 1 + i % (n - 1)).wait_send()
            return 0
        lax.fori_loop(0, PARTS * (n - 1), one, 0)

    def taps(y):
        main = [y[:, 256 * b : 256 * b + 256] for b in range(3)]
        left = [y[:, 768 + 64 * b : 832 + 64 * b] for b in range(3)]
        return main, left

    def conv_row(r):
        x = [xp[:, r + a].reshape(256, 320) for a in range(3)]
        y = dot(jnp.concatenate(x, axis=1), ws[...])
        pieces = []
        for f in range(2):
            main, left = taps(y[128 * f : 128 * f + 128])
            pieces.append([
                down(t[0], 1) + t[1] + up(t[2], 1) + b
                for t, b in ((main, bs[:, :256]), (left, bs[:, 256:]))
            ])

        def grouped(values):
            width = values[0].shape[1]
            both = [v.reshape(n, 2, 1, 8, width) for v in values]
            return [
                jnp.concatenate([both[0][:, g], both[1][:, g]], axis=1).reshape(n, 16, width)
                for g in range(2)
            ]

        main = grouped([pieces[0][0], pieces[1][0]])
        left = grouped([pieces[0][1], pieces[1][1]])
        for g in range(2):
            for half in range(2):
                snd[:, r, 2 * g + half] = main[g][:, :, 128 * half : 128 * half + 128].astype(BF16)
        snd[:, r, 4] = jnp.concatenate(left, axis=2).astype(BF16)

    lane = lax.broadcasted_iota(jnp.int32, (1, 128), 1)
    low = lane < HEAD
    same = lax.broadcasted_iota(jnp.int32, (8, 128), 0) == lax.broadcasted_iota(
        jnp.int32, (8, 128), 1
    ) % 8
    wall = jnp.where(same, 0.0, -1e30).astype(F32)

    def attend_row(r):
        m = 16 * n
        rest = rcv[:, r, 4].reshape(m, 128).astype(F32)
        xs = []
        for g in range(2):
            a = rcv[:, r, 2 * g].reshape(m, 128).astype(F32)
            b = rcv[:, r, 2 * g + 1].reshape(m, 128).astype(F32)
            own = rest if g == 0 else pltpu.roll(rest, 64, 1)
            xs.append(jnp.concatenate([a, b, own[:, :64]], axis=1))
        x = jnp.concatenate(xs, axis=0)
        y = dot(x.astype(BF16), wt[...])
        sums = []
        for g in range(2):
            main, left = taps(y[m * g : m * g + m])
            sums.append(jnp.concatenate(
                [down(t[0], 8) + t[1] + up(t[2], 8) for t in (main, left)], axis=1
            ))
        framed = (x + bt[...] + jnp.concatenate(sums, axis=0)).astype(BF16).astype(F32)
        center = jnp.sum(framed, axis=1, keepdims=True) * (1.0 / framed.shape[1])
        away = framed - center
        spread = jnp.sum(away * away, axis=1, keepdims=True) * (1.0 / framed.shape[1])
        normed = (away * lax.rsqrt(spread + 1e-05) * gain[...] + lbias[...]).astype(BF16)
        qkv = dot(normed, wqkv[...])
        ones = jnp.ones((m, 128), BF16)
        rows_out = []
        for g in range(2):
            part = qkv[m * g : m * g + m]

            def head(q, k, v):
                s = lax.dot_general(
                    q.astype(BF16), k, (((1,), (1,)), ((), ())), preferred_element_type=F32
                )
                s = (s.reshape(m // 8, 8, m) + wall[None]).reshape(m, m)
                e = jnp.exp(s - jnp.max(s, axis=1, keepdims=True)).astype(BF16)
                return dot(e, jnp.concatenate([v, ones], axis=1))

            cols = []
            for j in range(2):
                q = part[:, 128 * j : 128 * j + 128]
                k = part[:, 256 + 128 * j : 384 + 128 * j].astype(BF16)
                v = part[:, 512 + 128 * j : 640 + 128 * j].astype(BF16)
                even = head(jnp.where(low, q, 0.0), k, v)
                odd = head(jnp.where(low, 0.0, q), k, v)
                cols.append(
                    (jnp.where(low, even[:, :128], odd[:, :128])
                     / jnp.where(low, even[:, 128:], odd[:, 128:])).astype(BF16)
                )
            kv = part[:, 896:1024].astype(BF16)
            last = head(part[:, 768:896], kv, kv)
            cols.append((last[:, :128] / last[:, 128:]).astype(BF16))
            rows_out.append(jnp.concatenate(cols, axis=1))
        result = framed + dot(jnp.concatenate(rows_out, axis=0), wo[...]) + bo[...]
        lefts = []
        for g in range(2):
            part = result[m * g : m * g + m]
            for half in range(2):
                osnd[:, r, 2 * g + half] = (
                    part[:, 128 * half : 128 * half + 128].astype(BF16).reshape(n, 16, 128)
                )
            lefts.append(part[:, 256:])
        osnd[:, r, 4] = jnp.concatenate(lefts, axis=1).astype(BF16).reshape(n, 16, 128)

    def unpack_row(r):
        def pair(first, second):
            a = first.reshape(n, 2, 8, 128)
            b = second.reshape(n, 2, 8, 128)
            return [
                jnp.concatenate([a[:, f : f + 1], b[:, f : f + 1]], axis=1).reshape(16 * n, 128)
                for f in range(2)
            ]

        block = [orcv[:, r, i].astype(F32).reshape(16 * n, 128) for i in range(5)]
        for half in range(2):
            for f, value in enumerate(pair(block[half], block[2 + half])):
                out[f, r, :, 128 * half : 128 * half + 128] = value.astype(BF16)
        for f, value in enumerate(pair(block[4], pltpu.roll(block[4], 64, 1))):
            out[f, r, :, 256:320] = value[:, :64].astype(BF16)

    def each_row(part, body):
        def one(i, _):
            body(part * per + i)
            return 0
        lax.fori_loop(0, per, one, 0)

    def conv_part(i, _):
        part = lax.rem(i + 1, PARTS)

        @pl.when(i == PARTS - 2)
        def _():
            to_above.wait()
            to_below.wait()

            @pl.when(zi == 0)
            def _():
                xp[:, 0] = jnp.zeros((2,) + xp.shape[2:], BF16)

            @pl.when(zi == nrow - 1)
            def _():
                xp[:, rows + 1] = jnp.zeros((2,) + xp.shape[2:], BF16)

        each_row(part, conv_row)
        send_all(snd, rcv, s1, r1, part)
        return 0

    lax.fori_loop(0, PARTS, conv_part, 0)

    def attend_part(i, _):
        part = lax.rem(i + 1, PARTS)
        recv_all(snd, rcv, s1, r1, part)
        each_row(part, attend_row)
        send_all(osnd, orcv, s2, r2, part)
        return 0

    lax.fori_loop(0, PARTS, attend_part, 0)

    def unpack_part(i, _):
        part = lax.rem(i + 1, PARTS)
        recv_all(osnd, orcv, s2, r2, part)
        each_row(part, unpack_row)
        return 0

    lax.fori_loop(0, PARTS, unpack_part, 0)
    drain(snd, rcv, s1, r1)
    drain(osnd, orcv, s2, r2)


def taps_first(taps):
    return jnp.concatenate([t[:, :256] for t in taps] + [t[:, 256:] for t in taps], axis=1)


def fused_call(
    n, nrow, clip, w_spatial, b_spatial, w_temporal, b_temporal,
    ln_gain, ln_bias, w_query, w_key, w_value, w_out, b_out,
):
    width = clip.shape[3]
    rows = clip.shape[1]
    ws = taps_first([w_spatial[:, b].reshape(3 * width, width) for b in range(3)])
    wt = taps_first([w_temporal[k] for k in range(3)])
    wq = w_query * jnp.asarray(HEAD ** -0.5, BF16)
    wqkv = jnp.concatenate(
        [wq[:, :256], w_key[:, :256], w_value[:, :256], wq[:, 256:],
         jnp.zeros((width, 64), BF16), w_key[:, 256:], w_value[:, 256:]], axis=1,
    )
    wo = jnp.concatenate([w_out[:256], jnp.zeros((64, width), BF16), w_out[256:]], axis=0)
    vmem = pl.BlockSpec(memory_space=pltpu.VMEM)
    box = pltpu.VMEM((n, rows, 5, 16, 128), BF16)
    sems = pltpu.SemaphoreType.DMA((PARTS, n))
    return pl.pallas_call(
        functools.partial(fused, n, nrow),
        out_shape=jax.ShapeDtypeStruct(clip.shape, BF16),
        in_specs=[pl.BlockSpec(memory_space=pl.ANY)] + [vmem] * 9,
        out_specs=vmem,
        scratch_shapes=[
            pltpu.VMEM((2, rows + 2) + clip.shape[2:], BF16),
            box, box, box, box,
            pltpu.SemaphoreType.DMA,
            pltpu.SemaphoreType.DMA((2,)),
            pltpu.SemaphoreType.DMA((2,)),
            sems, sems, sems, sems,
        ],
        compiler_params=pltpu.CompilerParams(
            collective_id=0, has_side_effects=True, vmem_limit_bytes=48 * 1024 * 1024
        ),
        cost_estimate=pl.CostEstimate(
            flops=2 * 16 * width * width * clip.size // width,
            bytes_accessed=4 * clip.size, transcendentals=0,
        ),
    )(
        clip, ws, b_spatial[None], wt, b_temporal[None], ln_gain[None], ln_bias[None],
        wqkv, wo, b_out[None],
    )


def solution(mesh):
    n, nrow = mesh.shape["frame"], mesh.shape["row"]

    def body(clip, *weights):
        frames, rows, cols, width = clip.shape
        if (frames, cols, width, n) == (2, 128, 5 * HEAD, 8) and rows % PARTS == 0 and nrow > 2:
            return fused_call(n, nrow, clip, *weights)
        return on_device(clip, *weights)

    placed = (P("frame", "row", None, None), P(), P(), P(), P(), P(), P(), P(), P(), P(), P(), P())
    return jax.shard_map(
        body,
        mesh=mesh,
        in_specs=placed,
        out_specs=P("frame", "row", None, None),
        check_vma=False,
    )
```

profile of v0, /device:TPU:1, one launch (start us, length us, event | category | flops | bytes accessed | tf_op | source)
XLA Modules:
  0.0 81.8 jit_solution(14132328576313733126)
XLA Ops:
  0.0 0.8 broadcast_in_dim.21.bs
  0.8 0.7 broadcast_in_dim.22.bt
  1.5 0.7 broadcast_in_dim.23.gain
  2.2 0.7 broadcast_in_dim.24.lbias
  2.8 0.7 broadcast_in_dim.27.bo
  3.5 0.8 slice.103
  4.3 0.9 %slice.102 = bf16[256,320]{1,0:T(8,128)(2,1)S(1)} slice(bf16[320,320]{1,0:T(8,128)(2,1)} %param.22), slice={[0:256], [0:320]} | slice | bytes 327680 | tf_op jit(solution)/shard_map/slice | solution.py:392
  5.4 1.0 %broadcast_multiply_fusion = bf16[320,320]{1,0:T(8,128)(2,1)S(1)} fusion(bf16[320,320]{1,0:T(8,128)(2,1)} %param.19), kind=kLoop, calls=%fused_computation.4 | loop fusion | flops 102400 | bytes 409600 | tf_op jit(solution)/shard_map/mul | solution.py:387
  6.8 1.4 %slice_bitcast_fusion = (bf16[320,320]{1,0:T(8,128)(2,1)S(1)}, bf16[320,320]{1,0:T(8,128)(2,1)S(1)}, bf16[320,320]{1,0:T(8,128)(2,1)S(1)}) fusion(bf16[3,320,320]{2,1,0:T(8,128)(2,1)} %param.15), kind=kLoop, calls=%fused_computation.1 | loop fusion | bytes 1228800 | tf_op jit(solution)/shard_map/squeeze | solution.py:386
  8.2 0.6 slice.115
  9.5 0.7 slice.114
  10.2 0.7 slice.111
  10.9 1.9 %concatenate.13.wt = bf16[320,960]{1,0:T(8,128)(2,1)} concatenate(bf16[320,256]{1,0:T(8,128)(2,1)S(1)} %slice.110, bf16[320,256]{1,0:T(8,128)(2,1)} %slice.111, bf16[320,256]{1,0:T(8,128)(2,1)S(1)} %slice.112, bf16[320,64]{1,0:T(8,128)(2,1)} %slice.113, bf16[320,64]{1,0:T(8,128)(2,1)} %slice.114, bf16[320,64]{1,0:T(8,128)(2,1)} %slice.115), dimensions={1} | concatenate | bytes 1228800 | tf_op jit(solution)/shard_map/concatenate | solution.py:376
  13.0 0.7 slice.107
  13.8 0.7 slice.109
  14.5 0.8 slice.106
  15.3 0.7 slice.108
  16.0 0.8 slice.105
  16.8 3.9 %concatenate.12.ws = bf16[960,960]{1,0:T(8,128)(2,1)} concatenate(bf16[960,256]{1,0:T(8,128)(2,1)S(1)} %slice.104, bf16[960,256]{1,0:T(8,128)(2,1)} %slice.105, bf16[960,256]{1,0:T(8,128)(2,1)} %slice.106, bf16[960,64]{1,0:T(8,128)(2,1)} %slice.107, bf16[960,64]{1,0:T(8,128)(2,1)} %slice.108, bf16[960,64]{1,0:T(8,128)(2,1)} %slice.109), dimensions={1} | concatenate | bytes 3686400 | tf_op jit(solution)/shard_map/concatenate | solution.py:376
  20.7 2.4 %copy.13.clip = bf16[2,12,128,320]{3,2,1,0:T(8,128)(2,1)} copy(bf16[2,12,128,320]{2,3,1,0:T(8,128)(2,1)S(1)} %copy-done.3) | data formatting | bytes 3932160 | tf_op args[0]
  23.2 1.5 %copy-done = bf16[960,960]{1,0:T(8,128)(2,1)S(1)} copy-done((bf16[960,960]{1,0:T(8,128)(2,1)S(1)}, bf16[960,960]{1,0:T(8,128)(2,1)}, u32[]{:S(2)}) %copy-start) | copy-done | bytes 1843224
  24.7 1.1 %copy-done.1 = bf16[320,960]{1,0:T(8,128)(2,1)S(1)} copy-done((bf16[320,960]{1,0:T(8,128)(2,1)S(1)}, bf16[320,960]{1,0:T(8,128)(2,1)}, u32[]{:S(2)}) %copy-start.1) | copy-done | bytes 614424
  25.8 53.6 %shard_map.118 = bf16[2,12,128,320]{3,2,1,0:T(8,128)(2,1)S(1)} custom-call(bf16[2,12,128,320]{3,2,1,0:T(8,128)(2,1)} %copy.13.clip, bf16[960,960]{1,0:T(8,128)(2,1)S(1)} %copy-done, f32[1,320]{1,0:T(1,128)S(1)} %broadcast_in_dim.21.bs, bf16[320,960]{1,0:T(8,128)(2,1)S(1)} %copy-done.1, f32[1,320]{1,0:T(1,128)S(1)} %broadcast_in_dim.22.bt, ...), custom_call_target="tpu_custom_call" | custom-call | flops 10066329600 | bytes 3932160 | tf_op jit(solution)/shard_map/pallas_call | solution.py:396
  79.4 2.4 %copy.14 = bf16[2,12,128,320]{2,3,1,0:T(8,128)(2,1)} copy(bf16[2,12,128,320]{3,2,1,0:T(8,128)(2,1)S(1)} %shard_map.118) | data formatting | bytes 3932160 | tf_op jit(solution)/shard_map/pallas_call | solution.py:396
  (26 shorter events, 1.4 us)
Async XLA Ops:
  0.0 6.4 %slice-start.2 = ((bf16[320,320]{1,0:T(8,128)(2,1)}), bf16[320,64]{1,0:T(8,128)(2,1)S(1)}, s32[]{:S(2)}) async-start(bf16[320,320]{1,0:T(8,128)(2,1)} %param.21), calls=%async_computation.2 | async-start | bytes 163840 | tf_op jit(solution)/shard_map/slice | solution.py:390
  0.0 6.5 %slice-start.3 = ((bf16[320,320]{1,0:T(8,128)(2,1)}), bf16[320,256]{1,0:T(8,128)(2,1)S(1)}, s32[]{:S(2)}) async-start(bf16[320,320]{1,0:T(8,128)(2,1)} %param.21), calls=%async_computation.3 | async-start | bytes 327680 | tf_op jit(solution)/shard_map/slice | solution.py:389
  0.0 6.5 %slice-start = ((bf16[320,320]{1,0:T(8,128)(2,1)}), bf16[320,64]{1,0:T(8,128)(2,1)S(1)}, s32[]{:S(2)}) async-start(bf16[320,320]{1,0:T(8,128)(2,1)} %param.20), calls=%async_computation | async-start | bytes 163840 | tf_op jit(solution)/shard_map/slice | solution.py:390
  0.0 6.5 %slice-start.1 = ((bf16[320,320]{1,0:T(8,128)(2,1)}), bf16[320,256]{1,0:T(8,128)(2,1)S(1)}, s32[]{:S(2)}) async-start(bf16[320,320]{1,0:T(8,128)(2,1)} %param.20), calls=%async_computation.1 | async-start | bytes 327680 | tf_op jit(solution)/shard_map/slice | solution.py:389
  6.8 5.9 %copy-start.2 = (bf16[3,3,320,320]{3,2,1,0:T(8,128)(2,1)S(1)}, bf16[3,3,320,320]{3,2,1,0:T(8,128)(2,1)}, u32[]{:S(2)}) copy-start(bf16[3,3,320,320]{3,2,1,0:T(8,128)(2,1)} %param.13) | copy-start | bytes 5529604
  16.8 4.0 %copy-start.3 = (bf16[2,12,128,320]{2,3,1,0:T(8,128)(2,1)S(1)}, bf16[2,12,128,320]{2,3,1,0:T(8,128)(2,1)}, u32[]{:S(2)}) copy-start(bf16[2,12,128,320]{2,3,1,0:T(8,128)(2,1)} %param.12) | copy-start | bytes 5898244
  23.2 1.5 %copy-start = (bf16[960,960]{1,0:T(8,128)(2,1)S(1)}, bf16[960,960]{1,0:T(8,128)(2,1)}, u32[]{:S(2)}) copy-start(bf16[960,960]{1,0:T(8,128)(2,1)} %concatenate.12.ws) | copy-start | bytes 5529604
  24.7 1.1 %copy-start.1 = (bf16[320,960]{1,0:T(8,128)(2,1)S(1)}, bf16[320,960]{1,0:T(8,128)(2,1)}, u32[]{:S(2)}) copy-start(bf16[320,960]{1,0:T(8,128)(2,1)} %concatenate.13.wt) | copy-start | bytes 1843204
where the time goes:
time: 82.4 us; the launch traced here: 81.8 us
  Pallas kernels  53.6 us (65%)
  local copies, waits for them, and re-layouts  27 us (33%)
  other arithmetic  1.09 us (1%)
    pallas_call x1, Pallas kernels, fused_call(): pl.pallas_call(functools.partial(fused, n, nrow), out_shape=jax.ShapeDtyp...  53.6 us
    concatenate x2, local copies, waits for them, and re-layouts, taps_first(): jnp.concatenate([t[:, :256] for t in taps] + [t[:, 256:] for t in taps],...  5.82 us
    unnamed x9, local copies, waits for them, and re-layouts  5.08 us
    slice x6, local copies, waits for them, and re-layouts, taps_first(): t[:, 256:]  4.05 us
    pallas_call x1, local copies, waits for them, and re-layouts, fused_call(): pl.pallas_call(functools.partial(fused, n, nrow), out_shape=jax.ShapeDtyp...  2.4 us
    slice x6, local copies, waits for them, and re-layouts, taps_first(): t[:, :256]  2.34 us

commit v1 on v0

--- a/solution.py
+++ b/solution.py
@@ -130,8 +130,8 @@
 
 
 def fused(
-    n, nrow, clip, ws, bs, wt, bt, gain, lbias, wqkv, wo, bo, out,
-    xp, snd, rcv, osnd, orcv, load_sem, hsend, hrecv, s1, r1, s2, r2,
+    n, nrow, clip, wsp, wtp, wq, wk, wv, wo_in, vecs, out,
+    ws, wt, wqkv, wo, xp, snd, rcv, osnd, orcv, load_sem, hsend, hrecv, s1, r1, s2, r2,
 ):
     me = lax.axis_index("frame")
     zi = lax.axis_index("row")
@@ -142,6 +142,7 @@
 
     load = pltpu.make_async_copy(clip, xp.at[:, pl.ds(1, rows)], load_sem)
     load.start()
+    bs, bt, gain, lbias, bo = [vecs.at[pl.ds(i, 1)] for i in range(5)]
 
     barrier = pltpu.get_barrier_semaphore()
 
@@ -168,6 +169,31 @@
     )
     to_above.start()
     to_below.start()
+
+    def lay(target, first, count, parts):
+        for b, w in enumerate(parts):
+            target[first : first + count, 256 * b : 256 * b + 256] = w[:, :256]
+        left = [w[:, 256:].astype(F32) for w in parts]
+        target[first : first + count, 768:896] = jnp.concatenate(left[:2], axis=1).astype(BF16)
+        target[first : first + count, 896:960] = left[2].astype(BF16)
+
+    width = wq.shape[0]
+    for a in range(3):
+        lay(ws, width * a, width, [wsp[a, b] for b in range(3)])
+    lay(wt, 0, width, [wtp[k] for k in range(3)])
+    scaled = (wq[...].astype(F32) * HEAD ** -0.5).astype(BF16)
+    wqkv[:, :256] = scaled[:, :256]
+    wqkv[:, 256:512] = wk[:, :256]
+    wqkv[:, 512:768] = wv[:, :256]
+    wqkv[:, 768:896] = jnp.concatenate(
+        [scaled[:, 256:].astype(F32), jnp.zeros((width, 64), F32)], axis=1
+    ).astype(BF16)
+    wqkv[:, 896:1024] = jnp.concatenate(
+        [wk[:, 256:].astype(F32), wv[:, 256:].astype(F32)], axis=1
+    ).astype(BF16)
+    wo[:256] = wo_in[:256]
+    wo[256:320] = jnp.zeros((64, width), BF16)
+    wo[320:] = wo_in[256:]
     load.wait()
 
     def move(buf, land, ss, rs, part, k):
@@ -221,7 +247,7 @@
             main, left = taps(y[128 * f : 128 * f + 128])
             pieces.append([
                 down(t[0], 1) + t[1] + up(t[2], 1) + b
-                for t, b in ((main, bs[:, :256]), (left, bs[:, 256:]))
+                for t, b in ((main, bs[...][:, :256]), (left, bs[...][:, 256:]))
             ])
 
         def grouped(values):
@@ -372,33 +398,26 @@
     drain(osnd, orcv, s2, r2)
 
 
-def taps_first(taps):
-    return jnp.concatenate([t[:, :256] for t in taps] + [t[:, 256:] for t in taps], axis=1)
-
-
 def fused_call(
     n, nrow, clip, w_spatial, b_spatial, w_temporal, b_temporal,
     ln_gain, ln_bias, w_query, w_key, w_value, w_out, b_out,
 ):
     width = clip.shape[3]
     rows = clip.shape[1]
-    ws = taps_first([w_spatial[:, b].reshape(3 * width, width) for b in range(3)])
-    wt = taps_first([w_temporal[k] for k in range(3)])
-    wq = w_query * jnp.asarray(HEAD ** -0.5, BF16)
-    wqkv = jnp.concatenate(
-        [wq[:, :256], w_key[:, :256], w_value[:, :256], wq[:, 256:],
-         jnp.zeros((width, 64), BF16), w_key[:, 256:], w_value[:, 256:]], axis=1,
-    )
-    wo = jnp.concatenate([w_out[:256], jnp.zeros((64, width), BF16), w_out[256:]], axis=0)
+    vecs = jnp.stack([b_spatial, b_temporal, ln_gain, ln_bias, b_out])
     vmem = pl.BlockSpec(memory_space=pltpu.VMEM)
     box = pltpu.VMEM((n, rows, 5, 16, 128), BF16)
     sems = pltpu.SemaphoreType.DMA((PARTS, n))
     return pl.pallas_call(
         functools.partial(fused, n, nrow),
         out_shape=jax.ShapeDtypeStruct(clip.shape, BF16),
-        in_specs=[pl.BlockSpec(memory_space=pl.ANY)] + [vmem] * 9,
+        in_specs=[pl.BlockSpec(memory_space=pl.ANY)] + [vmem] * 7,
         out_specs=vmem,
         scratch_shapes=[
+            pltpu.VMEM((3 * width, 3 * width), BF16),
+            pltpu.VMEM((width, 3 * width), BF16),
+            pltpu.VMEM((width, 3 * width + 64), BF16),
+            pltpu.VMEM((width + 64, width), BF16),
             pltpu.VMEM((2, rows + 2) + clip.shape[2:], BF16),
             box, box, box, box,
             pltpu.SemaphoreType.DMA,
@@ -414,8 +433,7 @@
             bytes_accessed=4 * clip.size, transcendentals=0,
         ),
     )(
-        clip, ws, b_spatial[None], wt, b_temporal[None], ln_gain[None], ln_bias[None],
-        wqkv, wo, b_out[None],
+        clip, w_spatial, w_temporal, w_query, w_key, w_value, w_out, vecs,
     )
 
 

time: 82.4 us -> 70.1 us (0.85)
  local copies, waits for them, and re-layouts: 27 us -> 14 us
  Pallas kernels: 53.6 us -> 55.7 us
  other arithmetic: 1.09 us -> 0 us
    slice x25 -> x0, local copies, waits for them, and re-layouts: 8.4 us -> none  [the longest x6 4.05 us: taps_first(): t[:, 256:]]
    concatenate x4 -> x0, local copies, waits for them, and re-layouts: 6.16 us -> none  [the longest x2 5.82 us: taps_first(): jnp.concatenate([t[:, :256] for t in taps] + [t[:, 256:] for t in taps],...]
    another operation x0 -> x6, local copies, waits for them, and re-layouts: none -> 3.87 us  [fused_call(): vecs = jnp.stack([b_spatial, b_temporal, ln_gain, ln_bias, b_out])]
    broadcast_in_dim x7 -> x0, local copies, waits for them, and re-layouts: 3.5 us -> none  [the longest x1 0.75 us: fused_call(): b_spatial[None]]
    pallas_call x1, Pallas kernels: 53.6 us -> 55.7 us  [fused_call(): pl.pallas_call(functools.partial(fused, n, nrow), out_shape=jax.ShapeDtyp...]
    pallas_call x1, local copies, waits for them, and re-layouts: 2.4 us -> 4.14 us  [fused_call(): pl.pallas_call(functools.partial(fused, n, nrow), out_shape=jax.ShapeDtyp...]
    squeeze x1 -> x0, local copies, waits for them, and re-layouts: 1.41 us -> none  [fused_call(): wt = taps_first([w_temporal[k] for k in range(3)])]
    mul x1 -> x0, other arithmetic: 0.98 us -> none  [fused_call(): wq = w_query * jnp.asarray(HEAD ** (-0.5), BF16)]
where the time goes in v1:
time: 70.1 us; the launch traced here: 69.8 us
  Pallas kernels  55.7 us (79%)
  local copies, waits for them, and re-layouts  14 us (20%)
    pallas_call x1, Pallas kernels, fused_call(): pl.pallas_call(functools.partial(fused, n, nrow), out_shape=jax.ShapeDtyp...  55.7 us
    unnamed x13, local copies, waits for them, and re-layouts  6.01 us
    pallas_call x1, local copies, waits for them, and re-layouts, fused_call(): pl.pallas_call(functools.partial(fused, n, nrow), out_shape=jax.ShapeDtyp...  4.14 us
    another operation x6, local copies, waits for them, and re-layouts, fused_call(): vecs = jnp.stack([b_spatial, b_temporal, ln_gain, ln_bias, b_out])  3.87 us

profile of v1, /device:TPU:1, one launch (start us, length us, event | category | flops | bytes accessed | tf_op | source)
XLA Modules:
  0.0 69.8 jit_solution(11963994675608692165)
XLA Ops:
  0.0 0.0 copy-start.3
  0.0 0.0 copy-start.2
  0.0 0.0 copy-start.1
  0.0 0.0 copy-start
  0.0 0.8 %stack.18 = f32[1,320]{1,0:T(1,128)S(1)} reshape(f32[320]{0:T(512)} %param.14) | data formatting | bytes 2560 | tf_op jit(solution)/shard_map/stack | solution.py:407
  0.9 1.0 %stack.19 = f32[1,320]{1,0:T(1,128)S(1)} reshape(f32[320]{0:T(512)} %param.16) | data formatting | bytes 2560 | tf_op jit(solution)/shard_map/stack | solution.py:407
  1.8 0.7 stack.20
  2.5 0.7 stack.21
  3.2 0.7 stack.22
  3.9 4.1 %copy.13.clip = bf16[2,12,128,320]{3,2,1,0:T(8,128)(2,1)} copy(bf16[2,12,128,320]{2,3,1,0:T(8,128)(2,1)} %param.12) | data formatting | bytes 3932160 | tf_op args[0]
  8.0 0.0 copy-done.3
  8.0 0.0 copy-done.2
  8.0 0.0 copy-done.1
  8.0 0.0 copy-done
  8.0 0.0 copy-start.4
  8.0 0.9 %copy-done.4 = bf16[320,320]{1,0:T(8,128)(2,1)S(1)} copy-done((bf16[320,320]{1,0:T(8,128)(2,1)S(1)}, bf16[320,320]{1,0:T(8,128)(2,1)}, u32[]{:S(2)}) %copy-start.4) | copy-done | bytes 204824
  9.0 0.0 copy-start.5
  9.0 0.9 %copy-done.5 = bf16[320,320]{1,0:T(8,128)(2,1)S(1)} copy-done((bf16[320,320]{1,0:T(8,128)(2,1)S(1)}, bf16[320,320]{1,0:T(8,128)(2,1)}, u32[]{:S(2)}) %copy-start.5) | copy-done | bytes 204824
  9.9 55.7 %shard_map.118 = bf16[2,12,128,320]{3,2,1,0:T(8,128)(2,1)} custom-call(bf16[2,12,128,320]{3,2,1,0:T(8,128)(2,1)} %copy.13.clip, bf16[3,3,320,320]{3,2,1,0:T(8,128)(2,1)S(1)} %copy-done, bf16[3,320,320]{2,1,0:T(8,128)(2,1)S(1)} %copy-done.1, bf16[320,320]{1,0:T(8,128)(2,1)S(1)} %copy-done.2, bf16[320,320]{1,0:T(8,128)(2,1)S(1)} %copy-done.3, ...), custom_call_target="tpu_custom_call" | custom-call | flops 10066329600 | bytes 3932160 | tf_op jit(solution)/shard_map/pallas_call | solution.py:411
  65.6 4.1 %copy.14 = bf16[2,12,128,320]{2,3,1,0:T(8,128)(2,1)} copy(bf16[2,12,128,320]{3,2,1,0:T(8,128)(2,1)} %shard_map.118) | data formatting | bytes 3932160 | tf_op jit(solution)/shard_map/pallas_call | solution.py:411
  (1 shorter events, 0.0 us)
Async XLA Ops:
  0.0 8.0 %copy-start.3 = (bf16[320,320]{1,0:T(8,128)(2,1)S(1)}, bf16[320,320]{1,0:T(8,128)(2,1)}, u32[]{:S(2)}) copy-start(bf16[320,320]{1,0:T(8,128)(2,1)} %wk.1) | copy-start | bytes 614404
  0.0 8.0 %copy-start.2 = (bf16[320,320]{1,0:T(8,128)(2,1)S(1)}, bf16[320,320]{1,0:T(8,128)(2,1)}, u32[]{:S(2)}) copy-start(bf16[320,320]{1,0:T(8,128)(2,1)} %wq.1) | copy-start | bytes 614404
  0.0 8.0 %copy-start.1 = (bf16[3,320,320]{2,1,0:T(8,128)(2,1)S(1)}, bf16[3,320,320]{2,1,0:T(8,128)(2,1)}, u32[]{:S(2)}) copy-start(bf16[3,320,320]{2,1,0:T(8,128)(2,1)} %wtp.1) | copy-start | bytes 1843204
  0.0 8.0 %copy-start = (bf16[3,3,320,320]{3,2,1,0:T(8,128)(2,1)S(1)}, bf16[3,3,320,320]{3,2,1,0:T(8,128)(2,1)}, u32[]{:S(2)}) copy-start(bf16[3,3,320,320]{3,2,1,0:T(8,128)(2,1)} %wsp.1) | copy-start | bytes 5529604
  8.0 0.9 %copy-start.4 = (bf16[320,320]{1,0:T(8,128)(2,1)S(1)}, bf16[320,320]{1,0:T(8,128)(2,1)}, u32[]{:S(2)}) copy-start(bf16[320,320]{1,0:T(8,128)(2,1)} %wv.1) | copy-start | bytes 614404
  9.0 0.9 %copy-start.5 = (bf16[320,320]{1,0:T(8,128)(2,1)S(1)}, bf16[320,320]{1,0:T(8,128)(2,1)}, u32[]{:S(2)}) copy-start(bf16[320,320]{1,0:T(8,128)(2,1)} %wo_in.1) | copy-start | bytes 614404

commit v2 on v1

--- a/solution.py
+++ b/solution.py
@@ -240,8 +240,8 @@
         return main, left
 
     def conv_row(r):
-        x = [xp[:, r + a].reshape(256, 320) for a in range(3)]
-        y = dot(jnp.concatenate(x, axis=1), ws[...])
+        x = [xp[f, pl.ds(r, 3)].reshape(3 * width, 128).T for f in range(2)]
+        y = dot(jnp.concatenate(x, axis=0), ws[...])
         pieces = []
         for f in range(2):
             main, left = taps(y[128 * f : 128 * f + 128])
@@ -346,9 +346,9 @@
         block = [orcv[:, r, i].astype(F32).reshape(16 * n, 128) for i in range(5)]
         for half in range(2):
             for f, value in enumerate(pair(block[half], block[2 + half])):
-                out[f, r, :, 128 * half : 128 * half + 128] = value.astype(BF16)
+                out[f, r, 128 * half : 128 * half + 128] = value.T.astype(BF16)
         for f, value in enumerate(pair(block[4], pltpu.roll(block[4], 64, 1))):
-            out[f, r, :, 256:320] = value[:, :64].astype(BF16)
+            out[f, r, 256:320] = value.T[:64].astype(BF16)
 
     def each_row(part, body):
         def one(i, _):
@@ -404,13 +404,14 @@
 ):
     width = clip.shape[3]
     rows = clip.shape[1]
+    turned = jnp.swapaxes(clip, 2, 3)
     vecs = jnp.stack([b_spatial, b_temporal, ln_gain, ln_bias, b_out])
     vmem = pl.BlockSpec(memory_space=pltpu.VMEM)
     box = pltpu.VMEM((n, rows, 5, 16, 128), BF16)
     sems = pltpu.SemaphoreType.DMA((PARTS, n))
-    return pl.pallas_call(
+    result = pl.pallas_call(
         functools.partial(fused, n, nrow),
-        out_shape=jax.ShapeDtypeStruct(clip.shape, BF16),
+        out_shape=jax.ShapeDtypeStruct(turned.shape, BF16),
         in_specs=[pl.BlockSpec(memory_space=pl.ANY)] + [vmem] * 7,
         out_specs=vmem,
         scratch_shapes=[
@@ -418,7 +419,7 @@
             pltpu.VMEM((width, 3 * width), BF16),
             pltpu.VMEM((width, 3 * width + 64), BF16),
             pltpu.VMEM((width + 64, width), BF16),
-            pltpu.VMEM((2, rows + 2) + clip.shape[2:], BF16),
+            pltpu.VMEM((2, rows + 2) + turned.shape[2:], BF16),
             box, box, box, box,
             pltpu.SemaphoreType.DMA,
             pltpu.SemaphoreType.DMA((2,)),
@@ -433,8 +434,9 @@
             bytes_accessed=4 * clip.size, transcendentals=0,
         ),
     )(
-        clip, w_spatial, w_temporal, w_query, w_key, w_value, w_out, vecs,
-    )
+        turned, w_spatial, w_temporal, w_query, w_key, w_value, w_out, vecs,
+    )
+    return jnp.swapaxes(result, 2, 3)
 
 
 def solution(mesh):

time: 70.1 us -> 68.2 us (0.973)
  local copies, waits for them, and re-layouts: 14 us -> 11.1 us
  Pallas kernels: 55.7 us -> 56.6 us
    pallas_call x1 -> x0, local copies, waits for them, and re-layouts: 4.14 us -> none  [fused_call(): pl.pallas_call(functools.partial(fused, n, nrow), out_shape=jax.ShapeDtyp...]
    unnamed x13, local copies, waits for them, and re-layouts: 6.01 us -> 7.7 us
    pallas_call x1, Pallas kernels: 55.7 us -> 56.6 us  [fused_call(): pl.pallas_call(functools.partial(fused, n, nrow), out_shape=jax.ShapeDtyp...]
where the time goes in v2:
time: 68.2 us; the launch traced here: 67.8 us
  Pallas kernels  56.6 us (83%)
  local copies, waits for them, and re-layouts  11.1 us (16%)
    pallas_call x1, Pallas kernels, fused_call(): pl.pallas_call(functools.partial(fused, n, nrow), out_shape=jax.ShapeDtyp...  56.6 us
    unnamed x13, local copies, waits for them, and re-layouts  7.7 us
    another operation x6, local copies, waits for them, and re-layouts, fused_call(): vecs = jnp.stack([b_spatial, b_temporal, ln_gain, ln_bias, b_out])  3.44 us

profile of v2, /device:TPU:1, one launch (start us, length us, event | category | flops | bytes accessed | tf_op | source)
XLA Modules:
  0.0 67.8 jit_solution(2057156918858071175)
XLA Ops:
  0.0 0.7 %stack.18 = f32[1,320]{1,0:T(1,128)S(1)} reshape(f32[320]{0:T(512)} %param.14) | data formatting | bytes 2560 | tf_op jit(solution)/shard_map/stack | solution.py:408
  0.7 0.7 %stack.19 = f32[1,320]{1,0:T(1,128)S(1)} reshape(f32[320]{0:T(512)} %param.16) | data formatting | bytes 2560 | tf_op jit(solution)/shard_map/stack | solution.py:408
  1.4 0.7 %stack.20 = f32[1,320]{1,0:T(1,128)S(1)} reshape(f32[320]{0:T(512)} %param.17) | data formatting | bytes 2560 | tf_op jit(solution)/shard_map/stack | solution.py:408
  2.0 0.7 %stack.21 = f32[1,320]{1,0:T(1,128)S(1)} reshape(f32[320]{0:T(512)} %param.18) | data formatting | bytes 2560 | tf_op jit(solution)/shard_map/stack | solution.py:408
  2.7 0.7 %stack.22 = f32[1,320]{1,0:T(1,128)S(1)} reshape(f32[320]{0:T(512)} %param.23) | data formatting | bytes 2560 | tf_op jit(solution)/shard_map/stack | solution.py:408
  3.4 0.0 copy-start
  3.5 1.5 %copy-done = bf16[2,12,128,320]{2,3,1,0:T(8,128)(2,1)S(1)} copy-done((bf16[2,12,128,320]{2,3,1,0:T(8,128)(2,1)S(1)}, bf16[2,12,128,320]{2,3,1,0:T(8,128)(2,1)}, u32[]{:S(2)}) %copy-start) | copy-done | bytes 1966104
  5.0 0.0 copy-start.1
  5.0 1.1 %copy-done.1 = bf16[3,320,320]{2,1,0:T(8,128)(2,1)S(1)} copy-done((bf16[3,320,320]{2,1,0:T(8,128)(2,1)S(1)}, bf16[3,320,320]{2,1,0:T(8,128)(2,1)}, u32[]{:S(2)}) %copy-start.1) | copy-done | bytes 614424
  6.1 0.0 copy-start.2
  6.1 0.9 %copy-done.2 = bf16[320,320]{1,0:T(8,128)(2,1)S(1)} copy-done((bf16[320,320]{1,0:T(8,128)(2,1)S(1)}, bf16[320,320]{1,0:T(8,128)(2,1)}, u32[]{:S(2)}) %copy-start.2) | copy-done | bytes 204824
  7.0 0.0 copy-start.3
  7.1 0.9 %copy-done.3 = bf16[320,320]{1,0:T(8,128)(2,1)S(1)} copy-done((bf16[320,320]{1,0:T(8,128)(2,1)S(1)}, bf16[320,320]{1,0:T(8,128)(2,1)}, u32[]{:S(2)}) %copy-start.3) | copy-done | bytes 204824
  8.0 0.0 copy-start.4
  8.0 0.9 %copy-done.4 = bf16[320,320]{1,0:T(8,128)(2,1)S(1)} copy-done((bf16[320,320]{1,0:T(8,128)(2,1)S(1)}, bf16[320,320]{1,0:T(8,128)(2,1)}, u32[]{:S(2)}) %copy-start.4) | copy-done | bytes 204824
  8.9 0.0 copy-start.5
  8.9 0.9 %copy-done.5 = bf16[320,320]{1,0:T(8,128)(2,1)S(1)} copy-done((bf16[320,320]{1,0:T(8,128)(2,1)S(1)}, bf16[320,320]{1,0:T(8,128)(2,1)}, u32[]{:S(2)}) %copy-start.5) | copy-done | bytes 204824
  9.9 56.6 %shard_map.118 = bf16[2,12,320,128]{3,2,1,0:T(8,128)(2,1)S(1)} custom-call(bf16[2,12,320,128]{3,2,1,0:T(8,128)(2,1)S(1)} %bitcast.3, bf16[3,3,320,320]{3,2,1,0:T(8,128)(2,1)} %wsp.1, bf16[3,320,320]{2,1,0:T(8,128)(2,1)S(1)} %copy-done.1, bf16[320,320]{1,0:T(8,128)(2,1)S(1)} %copy-done.2, bf16[320,320]{1,0:T(8,128)(2,1)S(1)} %copy-done.3, ...), custom_call_target="tpu_custom_call" | custom-call | flops 10066329600 | bytes 3932160 | tf_op jit(solution)/shard_map/pallas_call | solution.py:412
  66.5 1.3 %copy.14 = bf16[2,12,128,320]{2,3,1,0:T(8,128)(2,1)} copy(bf16[2,12,128,320]{2,3,1,0:T(8,128)(2,1)S(1)} %bitcast.2) | data formatting | bytes 3932160
  (1 shorter events, 0.0 us)
Async XLA Ops:
  3.4 1.5 %copy-start = (bf16[2,12,128,320]{2,3,1,0:T(8,128)(2,1)S(1)}, bf16[2,12,128,320]{2,3,1,0:T(8,128)(2,1)}, u32[]{:S(2)}) copy-start(bf16[2,12,128,320]{2,3,1,0:T(8,128)(2,1)} %param.12) | copy-start | bytes 5898244
  5.0 1.1 %copy-start.1 = (bf16[3,320,320]{2,1,0:T(8,128)(2,1)S(1)}, bf16[3,320,320]{2,1,0:T(8,128)(2,1)}, u32[]{:S(2)}) copy-start(bf16[3,320,320]{2,1,0:T(8,128)(2,1)} %wtp.1) | copy-start | bytes 1843204
  6.1 0.9 %copy-start.2 = (bf16[320,320]{1,0:T(8,128)(2,1)S(1)}, bf16[320,320]{1,0:T(8,128)(2,1)}, u32[]{:S(2)}) copy-start(bf16[320,320]{1,0:T(8,128)(2,1)} %wq.1) | copy-start | bytes 614404
  7.0 0.9 %copy-start.3 = (bf16[320,320]{1,0:T(8,128)(2,1)S(1)}, bf16[320,320]{1,0:T(8,128)(2,1)}, u32[]{:S(2)}) copy-start(bf16[320,320]{1,0:T(8,128)(2,1)} %wk.1) | copy-start | bytes 614404
  8.0 0.9 %copy-start.4 = (bf16[320,320]{1,0:T(8,128)(2,1)S(1)}, bf16[320,320]{1,0:T(8,128)(2,1)}, u32[]{:S(2)}) copy-start(bf16[320,320]{1,0:T(8,128)(2,1)} %wv.1) | copy-start | bytes 614404
  8.9 0.9 %copy-start.5 = (bf16[320,320]{1,0:T(8,128)(2,1)S(1)}, bf16[320,320]{1,0:T(8,128)(2,1)}, u32[]{:S(2)}) copy-start(bf16[320,320]{1,0:T(8,128)(2,1)} %wo_in.1) | copy-start | bytes 614404
